TPU v7x, 32 devices: a whole 2x2x4 slice. The times are simulated.
32 devices in a mesh: sub: 4 (over z), cgrp: 8 (over y, x, core).
Axes of the slice: x: 2, y: 2, z: 4, core: 2. Of those that a mesh axis runs over, the one named last changes fastest.
Arguments:
- source: float32 [256, 32768], P('sub', 'cgrp'), may hold values from -7.5 to 7.5
- capacity: float32 [256, 32768], P('sub', 'cgrp'), may hold values from 0.01 to 1
- fd_weights: float32 [256, 32768], P('sub', 'cgrp'), may hold values from 0.02 to 1
- fd_modes: float32 [3, 64, 64], replicated, may hold values from -0.75 to 0.75
- face_modes: float32 [2, 128, 64], replicated, may hold values from -0.75 to 0.75
- coarse_map: int32 [4, 8, 6, 128], P('sub', 'cgrp'), may hold values from 0 to 24575, as said below
- fsai_cols: int32 [192, 8], P(('sub', 'cgrp')), may hold values from 0 to 191
- fsai_blocks: float32 [192, 8, 128, 128], P(('sub', 'cgrp')), may hold values from -0.1875 to 0.1875
Outputs:
- solution: float32 [256, 32768], P('sub', 'cgrp')
- residual: float32 [256, 32768], P('sub', 'cgrp')
Inputs may be any that keep to these rules, and one draw needn't show every extreme that they name: `coarse_map`: entries are numbered by owner: with d = s * 8 + t, face f of subdomain (s, t) takes the entries (6 d + f) * 128 to (6 d + f) * 128 + 127, each once, in an order of its own; except that face 0 of a subdomain with s > 0 takes exactly the entries of face 1 of subdomain (s - 1, t), and face 2 of a subdomain with t > 0 exactly those of face 3 of subdomain (s, t - 1), function k of both sides taking the same entry.
All inputs are finite; a program needn't handle non-finite values.
Results may differ from a plain program's by a relative error of at most 0.0001.
Values sent between devices are 32-bit elements; how exact they have to be, the bound alone decides.
A program may use at most 64 MiB of HBM per device.

v0:
```python
import jax
import jax.numpy as jnp
from jax import lax
from jax.sharding import PartitionSpec as P

C = 64
highest = lax.Precision.HIGHEST
along_first = 1.0
along_second = 0.6
along_third = 2.5


def with_halo(array, sides, width):
    for axis, dim in sides:
        count, length = (lax.axis_size(axis), array.shape[dim])
        up = [(i, (i + 1) % count) for i in range(count - 1)]
        down = [(j, i) for i, j in up]
        last = lax.slice_in_dim(array, length - width, length, axis=dim)
        first = lax.slice_in_dim(array, 0, width, axis=dim)
        before = lax.ppermute(last, axis, up)
        after = lax.ppermute(first, axis, down)
        array = jnp.concatenate([before, array, after], axis=dim)
    return array


def operate(field, capacity):
    padded = with_halo(field, (("sub", 0), ("cgrp", 1)), 1)
    padded = jnp.pad(padded, ((0, 0), (0, 0), (1, 1)))
    first = padded[2:, 1:-1, 1:-1] + padded[:-2, 1:-1, 1:-1]
    second = padded[1:-1, 2:, 1:-1] + padded[1:-1, :-2, 1:-1]
    third = padded[1:-1, 1:-1, 2:] + padded[1:-1, 1:-1, :-2]
    diagonal = capacity + 2.0 * (along_first + along_second + along_third)
    return diagonal * field - along_first * first - along_second * second - along_third * third


def transform(blocks, modes):
    blocks = jnp.einsum("ai,...ijk->...ajk", modes[0], blocks, precision=highest)
    blocks = jnp.einsum("bj,...ajk->...abk", modes[1], blocks, precision=highest)
    return jnp.einsum("ck,...abk->...abc", modes[2], blocks, precision=highest)


def transform_back(blocks, modes):
    blocks = jnp.einsum("ai,...ajk->...ijk", modes[0], blocks, precision=highest)
    blocks = jnp.einsum("bj,...ibk->...ijk", modes[1], blocks, precision=highest)
    return jnp.einsum("ck,...ijc->...ijk", modes[2], blocks, precision=highest)


def face_planes(blocks):
    return jnp.stack(
        [
            blocks[..., 0, :, :],
            blocks[..., -1, :, :],
            blocks[..., :, 0, :],
            blocks[..., :, -1, :],
            blocks[..., :, :, 0],
            blocks[..., :, :, -1],
        ],
        axis=-3,
    )


def restrict(planes, face_modes):
    partial_rows = jnp.einsum("ka,...fab->...fkb", face_modes[0], planes, precision=highest)
    return jnp.sum(partial_rows * face_modes[1], axis=-1)


def extend(values, face_modes):
    return jnp.einsum(
        "ka,...fkb->...fab", face_modes[0], values[..., None] * face_modes[1], precision=highest
    )


def add_planes(blocks, planes):
    blocks = blocks.at[..., 0, :, :].add(planes[..., 0, :, :])
    blocks = blocks.at[..., -1, :, :].add(planes[..., 1, :, :])
    blocks = blocks.at[..., :, 0, :].add(planes[..., 2, :, :])
    blocks = blocks.at[..., :, -1, :].add(planes[..., 3, :, :])
    blocks = blocks.at[..., :, :, 0].add(planes[..., 4, :, :])
    blocks = blocks.at[..., :, :, -1].add(planes[..., 5, :, :])
    return blocks


def coarse_apply(coarse, fsai_cols, fsai_blocks):
    table = coarse.reshape(-1, fsai_blocks.shape[2])
    picked = table[fsai_cols]
    image = jnp.einsum("rnij,rnj->ri", fsai_blocks, picked, precision=highest)
    spread = jnp.einsum("rnij,ri->rnj", fsai_blocks, image, precision=highest)
    return jnp.zeros_like(table).at[fsai_cols].add(spread).reshape(-1)


def coarse_round(coarse_local, coarse_map, fsai_cols, fsai_blocks):
    slots = coarse_map.reshape(-1)
    length = fsai_blocks.shape[0] * fsai_blocks.shape[2] * lax.axis_size(("sub", "cgrp"))
    term = jnp.zeros((length,), jnp.float32).at[slots].add(coarse_local.reshape(-1))
    coarse = lax.psum(term, ("sub", "cgrp"))
    back = lax.psum(coarse_apply(coarse, fsai_cols, fsai_blocks), ("sub", "cgrp"))
    return back[slots].reshape(coarse_local.shape)


def precondition(residual, fd_weights, fd_modes, face_modes, coarse_map, fsai_cols, fsai_blocks):
    local = transform_back(fd_weights * transform(residual, fd_modes), fd_modes)
    coarse_local = restrict(face_planes(residual), face_modes)
    correction = coarse_round(coarse_local, coarse_map, fsai_cols, fsai_blocks)
    return add_planes(local, extend(correction, face_modes))


def inner_sum(left, right):
    return lax.psum(jnp.sum(left * right), ("sub", "cgrp"))


def curvature_sum(left, right):
    return lax.psum(jnp.sum(left * right), ("sub", "cgrp"))


def body(source, capacity, fd_weights, fd_modes, face_modes, coarse_map, fsai_cols, fsai_blocks):
    cube = (C, C, C)
    flat_shape = source.shape
    source = source.reshape(cube)
    capacity = capacity.reshape(cube)
    fd_weights = fd_weights.reshape(cube)
    residual = source
    precond = precondition(
        residual, fd_weights, fd_modes, face_modes, coarse_map, fsai_cols, fsai_blocks
    )
    gamma = inner_sum(residual, precond)
    image = operate(precond, capacity)
    alpha = gamma / curvature_sum(precond, image)
    solution = alpha * precond
    residual = residual - alpha * image
    return (solution.reshape(flat_shape), residual.reshape(flat_shape))


def solution(mesh):
    in_specs = (
        P("sub", "cgrp"),
        P("sub", "cgrp"),
        P("sub", "cgrp"),
        P(),
        P(),
        P("sub", "cgrp", None, None),
        P(("sub", "cgrp"), None),
        P(("sub", "cgrp"), None, None, None),
    )
    out_specs = (P("sub", "cgrp"), P("sub", "cgrp"))
    return jax.shard_map(body, mesh=mesh, in_specs=in_specs, out_specs=out_specs, check_vma=False)
```

profile of v0, /device:TPU:0, one launch (start us, length us, event | category | flops | bytes accessed | tf_op | source)
XLA Modules:
  0.0 433.0 jit_solution(17539706606090331872)
XLA Ops:
  7.2 1.2 slice_reduce_fusion
  8.4 3.1 reshape.238
  11.5 1.7 fusion.60
  13.2 5.0 %fusion.59 = (f32[64,64,1]{2,1,0:T(8,128)}, f32[64,64,1]{2,1,0:T(8,128)}) fusion(f32[64,64,64]{2,1,0:T(8,128)} %reshape.238), kind=kLoop, calls=%fused_computation.103 | loop fusion | bytes 65536 | tf_op jit(solution)/shard_map/slice | solution.py:56
  18.3 0.7 copy.89
  19.2 1.5 copy.122
  20.6 0.7 copy.121
  21.4 3.3 copy.124
  24.6 3.2 copy.123
  27.8 0.8 constant_dynamic-update-slice_fusion
  28.6 0.8 bitcast_dynamic-update-slice_fusion.3
  29.4 0.8 bitcast_dynamic-update-slice_fusion.2
  30.1 0.8 bitcast_dynamic-update-slice_fusion.1
  30.9 0.8 bitcast_dynamic-update-slice_fusion
  31.6 0.3 fusion.25
  32.0 6.5 %scatter_custom_fusion = f32[24576]{0:T(1024)} fusion(s32[768]{0:T(1024)S(1)} %fusion.53, f32[768]{0:T(1024)S(1)} %bitcast.105, f32[]{:T(128)} %constant.167.clone.1), kind=kCustom, calls=%fused_computation.52 | custom fusion | flops 768 | bytes 98308 | tf_op jit(solution)/shard_map/scatter-add | solution.py:94
  38.5 0.6 all-reduce.7.cloned.1.call-start
  39.2 4.6 %fusion.16 = f32[64,64,64]{2,0,1:T(8,128)S(1)} fusion(f32[64,64,64]{2,1,0:T(8,128)} %reshape.238, f32[3,64,64]{2,1,0:T(8,128)S(1)} %copy-done.7), kind=kOutput, calls=%fused_computation.36 | convolution fusion | flops 201326592 | bytes 2129920 | tf_op jit(solution)/shard_map/ai,...ijk->...ajk/dot_general | solution.py:37
  43.7 5.6 %fusion.14 = f32[64,64,64]{2,1,0:T(8,128)} fusion(f32[64,64,64]{2,0,1:T(8,128)S(1)} %fusion.16, f32[3,64,64]{2,1,0:T(8,128)S(1)} %copy-done.7), kind=kOutput, calls=%fused_computation.34 | convolution fusion | flops 201326592 | bytes 3178496 | tf_op jit(solution)/shard_map/bj,...ajk->...abk/dot_general | solution.py:38
  49.3 3.3 reshape.239
  52.6 5.8 %fusion.21 = f32[64,64,64]{2,1,0:T(8,128)S(1)} fusion(f32[64,64,64]{2,1,0:T(8,128)} %reshape.239, f32[64,64,64]{2,1,0:T(8,128)} %fusion.14, f32[3,64,64]{2,1,0:T(8,128)S(1)} %copy-done.7), kind=kOutput, calls=%fused_computation.42 | convolution fusion | flops 201588736 | bytes 3178496 | tf_op jit(solution)/shard_map/ck,...abk->...abc/dot_general | solution.py:39
  58.4 5.6 %fusion.18 = f32[64,64,64]{0,2,1:T(8,128)} fusion(f32[64,64,64]{2,1,0:T(8,128)S(1)} %fusion.21, f32[3,64,64]{2,1,0:T(8,128)S(1)} %copy-done.7), kind=kOutput, calls=%fused_computation.41 | convolution fusion | flops 201326592 | bytes 3178496 | tf_op jit(solution)/shard_map/ai,...ajk->...ijk/dot_general | solution.py:43
  64.0 4.3 %copy.80 = f32[64,64,64]{1,2,0:T(8,128)} copy(f32[64,64,64]{0,2,1:T(8,128)} %fusion.18) | data formatting | bytes 2097152 | tf_op jit(solution)/shard_map/ai,...ajk->...ijk/dot_general | solution.py:43
  68.4 3.5 fusion.40
  71.8 3.4 fusion.8
  75.2 86.7 %all-reduce.5.cloned.1.call-done = f32[192,128]{1,0:T(8,128)} async-done(((f32[192,128]{1,0:T(8,128)}), f32[192,128]{1,0:T(8,128)}) %all-reduce.5.cloned.1.call-update) | async-done | bytes 98320 | tf_op jit(solution)/shard_map/psum | solution.py:95
  161.9 1.5 gather_fusion
  163.4 2.7 fusion.62
  166.1 1.6 fusion.54
  167.7 1.4 scatter_custom_fusion.1
  169.2 121.4 %all-reduce.7.cloned.1.call-done = f32[24576]{0:T(1024)} async-done(((f32[24576]{0:T(1024)}), f32[24576]{0:T(1024)}) %all-reduce.7.cloned.1.call-update) | async-done | bytes 98320 | tf_op jit(solution)/shard_map/psum | solution.py:96
  290.6 5.0 %gather_fusion.1 = f32[768]{0:T(1024)S(1)} fusion(f32[24576]{0:T(1024)} %all-reduce.7.cloned.1.call-done, s32[1024]{0:T(1024)S(1)} %pad_clamp_fusion), kind=kCustom, calls=%fused_computation.1 | custom fusion | bytes 9216 | tf_op jit(solution)/shard_map/gather | solution.py:97
  295.6 0.7 convolution_bitcast_fusion
  296.6 0.7 copy.126
  297.3 2.1 copy.95
  299.4 5.1 %scatter-add.48 = f32[64,64,64]{1,2,0:T(8,128)S(1)} dynamic-update-slice(f32[64,64,64]{1,2,0:T(8,128)S(1)} %constant_dynamic-update-slice_fusion.2, f32[64,1,64]{1,2,0:T(8,128)} %copy.95, s32[]{:T(128)} %constant.168.clone.1, s32[]{:T(128)} %constant.168.clone.1, s32[]{:T(128)} %constant.168.clone.1) | dynamic-update-slice | bytes 32772 | tf_op jit(solution)/shard_map/scatter-add | solution.py:76
  304.4 2.0 slice.283
  306.4 2.3 copy.127
  308.7 2.1 copy.97
  310.7 8.4 %scatter-add.49 = f32[64,64,64]{1,2,0:T(8,128)S(1)} dynamic-update-slice(f32[64,64,64]{1,2,0:T(8,128)S(1)} %scatter-add.48, f32[64,1,64]{1,2,0:T(8,128)} %copy.97, s32[]{:T(128)} %constant.168.clone.1, s32[]{:T(128)} %constant.171.clone.1, s32[]{:T(128)} %constant.168.clone.1) | dynamic-update-slice | bytes 32772 | tf_op jit(solution)/shard_map/scatter-add | solution.py:77
  319.6 5.1 %collective-permute-start.1 = (f32[1,64,64]{1,2,0:T(8,128)S(1)}, f32[1,64,64]{1,2,0:T(8,128)S(1)}, u32[]{:S(2)}, u32[]{:S(2)}) collective-permute-start(f32[1,64,64]{1,2,0:T(8,128)S(1)} %get-tuple-element.83), channel_id=1, source_target_pairs={{0,8},{8,16},{16,24},{1,9},{9,17},{17,25},{2,10},{10,18},{18,26},{... | collective-permute-start | bytes 49160 | tf_op jit(solution)/shard_map/ppermute | solution.py:20
  324.8 1.3 collective-permute-start
  326.3 4.2 collective-permute-done
  330.8 2.8 fusion.57
  333.5 2.8 copy.104
  336.3 2.8 copy.102
  339.1 1.3 collective-permute-start.2
  340.4 3.0 collective-permute-start.3
  343.4 1.3 broadcast_add_fusion
  344.7 3.1 copy.100
  347.8 2.2 add.99
  350.0 2.9 copy.101
  353.0 3.0 copy.105
  356.0 3.1 copy.103
  359.1 3.7 select_maximum_fusion
  362.8 0.4 copy-done.5
  363.3 0.6 copy-done.6
  363.9 6.5 %multiply_reduce_fusion = (f32[]{:T(128)}, f32[]{:T(128)}, f32[64,64,64]{1,2,0:T(8,128)}) fusion(f32[64,64,64]{1,2,0:T(8,128)S(1)} %scatter-add.51, f32[64,64,64]{1,2,0:T(8,128)S(1)} %copy-done.5, f32[66,66,66]{1,2,0:T(8,128)S(1)} %select_maximum_fusion, f32[1,64,64]{1,2,0:T(8,128)S(1)} %collective-permute-done, f32[1,64,64]{1,2,0:T(8,128)S(1)} %collective-permute-done.1, ...), kind=kLoop, calls=%fused_computation.39 | loop fusion | flops 5505022 | bytes 6358024 | tf_op jit(solution)/shard_map/reduce_sum | solution.py:112
  370.4 39.3 %all-reduce.1 = (f32[]{:T(128)}, f32[]{:T(128)}) all-reduce(f32[]{:T(128)} %get-tuple-element.75, f32[]{:T(128)} %get-tuple-element.74), channel_id=1, replica_groups=mesh['sub'=4,'cgrp'=8] {'sub','cgrp'}, use_global_device_ids=true, to_apply=%region_6.0 | all-reduce | flops 2 | bytes 16 | tf_op jit(solution)/shard_map/psum | solution.py:108
  411.1 5.4 %multiply_subtract_fusion = (f32[64,64,64]{1,2,0:T(8,128)}, f32[64,64,64]{1,2,0:T(8,128)}) fusion(f32[64,64,64]{1,2,0:T(8,128)} %copy.100, f32[64,64,64]{1,2,0:T(8,128)} %get-tuple-element.80, f32[]{:T(128)S(6)} %div.3, f32[64,64,64]{1,2,0:T(8,128)S(1)} %scatter-add.51), kind=kLoop, calls=%fused_computation.38 | loop fusion | flops 786432 | bytes 5242884 | tf_op jit(solution)/shard_map/sub | solution.py:129
  416.4 1.9 copy.110
  418.4 1.6 reshape.249
  420.0 3.1 copy.108
  423.1 2.9 reshape.248
  (57 shorter events, 1.7 us)
Async XLA Ops:
  7.2 156.2 %copy-start = (f32[6,8,128,128]{3,2,1,0:T(8,128)S(1)}, f32[6,8,128,128]{3,2,1,0:T(8,128)}, u32[]{:S(2)}) copy-start(f32[6,8,128,128]{3,2,1,0:T(8,128)} %param.27) | copy-start | bytes 9437188
  7.2 154.7 %all-reduce.5.cloned.1.call-start = ((), (), s32[]{:S(2)}) async-start(), calls=%async_computation | async-start | bytes 196608 | tf_op jit(solution)/shard_map/psum | solution.py:95
  13.2 5.0 %copy-start.10 = (s32[1,1,6,128]{3,1,2,0:T(1,128)S(1)}, s32[1,1,6,128]{3,1,2,0:T(1,128)}, u32[]{:S(2)}) copy-start(s32[1,1,6,128]{3,1,2,0:T(1,128)} %param.25) | copy-start | bytes 9220
  13.2 5.0 %copy-start.8 = (f32[2,128,64]{1,2,0:T(8,128)S(1)}, f32[2,128,64]{1,2,0:T(8,128)}, u32[]{:S(2)}) copy-start(f32[2,128,64]{1,2,0:T(8,128)} %param.24) | copy-start | bytes 196612
  21.3 17.7 %copy-start.9 = (s32[6,8]{1,0:T(8,128)S(1)}, s32[6,8]{1,0:T(8,128)}, u32[]{:S(2)}) copy-start(s32[6,8]{1,0:T(8,128)} %param.26) | copy-start | bytes 580
  21.3 17.8 %copy-start.7 = (f32[3,64,64]{2,1,0:T(8,128)S(1)}, f32[3,64,64]{2,1,0:T(8,128)}, u32[]{:S(2)}) copy-start(f32[3,64,64]{2,1,0:T(8,128)} %param.23) | copy-start | bytes 147460
  38.5 252.1 %all-reduce.7.cloned.1.call-start = ((), (), s32[]{:S(2)}) async-start(), calls=%async_computation.1 | async-start | bytes 196608 | tf_op jit(solution)/shard_map/psum | solution.py:96
  166.1 3.0 slice-start
  169.1 127.3 %copy-start.2 = (f32[64,64,64]{1,2,0:T(8,128)S(1)}, f32[64,64,64]{1,2,0:T(8,128)}, u32[]{:S(2)}) copy-start(f32[64,64,64]{1,2,0:T(8,128)} %fusion.8) | copy-start | bytes 3145732
  319.6 6.7 %collective-permute-start.1 = (f32[1,64,64]{1,2,0:T(8,128)S(1)}, f32[1,64,64]{1,2,0:T(8,128)S(1)}, u32[]{:S(2)}, u32[]{:S(2)}) collective-permute-start(f32[1,64,64]{1,2,0:T(8,128)S(1)} %get-tuple-element.83), channel_id=1, source_target_pairs={{0,8},{8,16},{16,24},{1,9},{9,17},{17,25},{2,10},{10,18},{18,26},{... | collective-permute-start | bytes 49160 | tf_op jit(solution)/shard_map/ppermute | solution.py:20
  324.8 5.8 %collective-permute-start = (f32[1,64,64]{1,2,0:T(8,128)S(1)}, f32[1,64,64]{1,2,0:T(8,128)S(1)}, u32[]{:S(2)}, u32[]{:S(2)}) collective-permute-start(f32[1,64,64]{1,2,0:T(8,128)S(1)} %get-tuple-element.84), channel_id=1, source_target_pairs={{8,0},{16,8},{24,16},{9,1},{17,9},{25,17},{10,2},{18,10},{26,18},{... | collective-permute-start | bytes 49160 | tf_op jit(solution)/shard_map/ppermute | solution.py:21
  339.1 16.9 %collective-permute-start.2 = (f32[66,1,64]{0,2,1:T(8,128)S(1)}, f32[66,1,64]{0,2,1:T(8,128)S(1)}, u32[]{:S(2)}, u32[]{:S(2)}) collective-permute-start(f32[66,1,64]{0,2,1:T(8,128)S(1)} %copy.102), channel_id=1, source_target_pairs={{1,0},{2,1},{3,2},{4,3},{5,4},{6,5},{7,6},{9,8},{10,9},{11,10},{12... | collective-permute-start | bytes 50696 | tf_op jit(solution)/shard_map/ppermute | solution.py:21
  340.4 12.6 %collective-permute-start.3 = (f32[66,1,64]{0,2,1:T(8,128)S(1)}, f32[66,1,64]{0,2,1:T(8,128)S(1)}, u32[]{:S(2)}, u32[]{:S(2)}) collective-permute-start(f32[66,1,64]{0,2,1:T(8,128)S(1)} %copy.104), channel_id=1, source_target_pairs={{0,1},{1,2},{2,3},{3,4},{4,5},{5,6},{6,7},{8,9},{9,10},{10,11},{11... | collective-permute-start | bytes 50696 | tf_op jit(solution)/shard_map/ppermute | solution.py:20
  359.1 3.8 copy-start.3
  359.1 3.8 copy-start.4
  359.1 4.2 copy-start.5
  359.1 4.8 %copy-start.6 = (f32[64,64,64]{1,2,0:T(8,128)S(1)}, f32[64,64,64]{1,2,0:T(8,128)}, u32[]{:S(2)}) copy-start(f32[64,64,64]{1,2,0:T(8,128)} %copy.101) | copy-start | bytes 3145732
  420.0 6.0 %copy-start.1 = (f32[6,8,128,128]{3,2,1,0:T(8,128)S(1)}, f32[6,8,128,128]{3,2,1,0:T(8,128)}, u32[]{:S(2)}) copy-start(f32[6,8,128,128]{3,2,1,0:T(8,128)} %param.27) | copy-start | bytes 9437188
Sparse Core Ops, SparseCore 0:
  38.6 123.2 all-reduce.4
  169.2 121.3 all-reduce.6
where the time goes:
time: 439 us; the launch traced here: 433 us
  waiting for transfers between devices  213 us (49%)
  local copies, waits for them, and re-layouts  94.9 us (22%)
  blocking collectives  39.3 us (9%)
  matrix products  33.6 us (8%)
  other arithmetic  25.1 us (6%)
  between operations  15.9 us (4%)
  starting transfers between devices  11.4 us (3%)
    psum x1, waiting for transfers between devices, coarse_round(): lax.psum(coarse_apply(coarse, fsai_cols, fsai_blocks), ('sub', 'cgrp'))  121 us
    psum x1, waiting for transfers between devices, coarse_round(): coarse = lax.psum(term, ('sub', 'cgrp'))  86.7 us
    psum x1, blocking collectives, inner_sum(): return lax.psum(jnp.sum(left * right), ('sub', 'cgrp'))  39.3 us
    unnamed x35, local copies, waits for them, and re-layouts  15.9 us
  transfers between devices with their start and end apart: 6, of which 4 were waited for; matrix products, arithmetic and copies ran while one was open for 11% of the time, Pallas kernels for 0%

commit v1 on v0

--- a/solution.py
+++ b/solution.py
@@ -93,7 +93,10 @@
     length = fsai_blocks.shape[0] * fsai_blocks.shape[2] * lax.axis_size(("sub", "cgrp"))
     term = jnp.zeros((length,), jnp.float32).at[slots].add(coarse_local.reshape(-1))
     coarse = lax.psum(term, ("sub", "cgrp"))
-    back = lax.psum(coarse_apply(coarse, fsai_cols, fsai_blocks), ("sub", "cgrp"))
+    convert_node = lambda inner_x, chip_axis, axis_tag: lax.psum(
+        lax.psum(inner_x, chip_axis), axis_tag
+    )
+    back = convert_node(coarse_apply(coarse, fsai_cols, fsai_blocks), "cgrp", "sub")
     return back[slots].reshape(coarse_local.shape)
 
 

time: 439 us -> 406 us (0.925)
  waiting for transfers between devices: 213 us -> 180 us
    psum x1 -> x2, waiting for transfers between devices: 121 us -> 86.3 us  [the longest x1 48.9 us: coarse_round(): lax.psum(inner_x, chip_axis)]
    unnamed x35 -> x33, local copies, waits for them, and re-layouts: 15.9 us -> 15.9 us
  transfers between devices with their start and end apart: 6 -> 7, of which waited for: 4 -> 5; matrix products, arithmetic and copies ran while one was open for 11% -> 13% of each run, Pallas kernels for 0% -> 0%
where the time goes in v1:
time: 406 us; the launch traced here: 400 us
  waiting for transfers between devices  180 us (44%)
  local copies, waits for them, and re-layouts  94.9 us (23%)
  blocking collectives  40.2 us (10%)
  matrix products  35.1 us (9%)
  other arithmetic  25.1 us (6%)
  between operations  15.6 us (4%)
  starting transfers between devices  9.53 us (2%)
    psum x1, waiting for transfers between devices, coarse_round(): coarse = lax.psum(term, ('sub', 'cgrp'))  88.8 us
    psum x1, waiting for transfers between devices, coarse_round(): lax.psum(inner_x, chip_axis)  48.9 us
    psum x1, blocking collectives, inner_sum(): return lax.psum(jnp.sum(left * right), ('sub', 'cgrp'))  40.2 us
    psum x1, waiting for transfers between devices, coarse_round(): lax.psum(lax.psum(inner_x, chip_axis), axis_tag)  37.5 us
    unnamed x33, local copies, waits for them, and re-layouts  15.9 us
    scatter-add x1, local copies, waits for them, and re-layouts, add_planes(): blocks = blocks.at[..., :, -1, :].add(planes[..., 3, :, :])  8.36 us
  transfers between devices with their start and end apart: 7, of which 5 were waited for; matrix products, arithmetic and copies ran while one was open for 13% of the time, Pallas kernels for 0%

profile of v1, /device:TPU:0, one launch (start us, length us, event | category | flops | bytes accessed | tf_op | source)
XLA Modules:
  0.0 400.1 jit_solution(4953499786821430908)
XLA Ops:
  7.2 1.2 slice_reduce_fusion
  8.4 3.1 reshape.238
  11.5 1.7 fusion.60
  13.2 5.0 %fusion.59 = (f32[64,64,1]{2,1,0:T(8,128)}, f32[64,64,1]{2,1,0:T(8,128)}) fusion(f32[64,64,64]{2,1,0:T(8,128)} %reshape.238), kind=kLoop, calls=%fused_computation.103 | loop fusion | bytes 65536 | tf_op jit(solution)/shard_map/slice | solution.py:56
  18.3 0.7 copy.89
  19.2 1.5 copy.122
  20.6 0.7 copy.121
  21.4 3.3 copy.124
  24.6 3.2 copy.123
  27.8 0.8 constant_dynamic-update-slice_fusion
  28.6 0.8 bitcast_dynamic-update-slice_fusion.3
  29.4 0.8 bitcast_dynamic-update-slice_fusion.2
  30.1 0.8 bitcast_dynamic-update-slice_fusion.1
  30.9 0.8 bitcast_dynamic-update-slice_fusion
  32.0 6.5 %scatter_custom_fusion = f32[24576]{0:T(1024)} fusion(s32[768]{0:T(1024)S(1)} %fusion.53, f32[768]{0:T(1024)S(1)} %bitcast.105, f32[]{:T(128)} %constant.167.clone.1), kind=kCustom, calls=%fused_computation.52 | custom fusion | flops 768 | bytes 98308 | tf_op jit(solution)/shard_map/scatter-add | solution.py:94
  38.5 0.6 all-reduce.8.cloned.1.call-start
  39.2 4.6 %fusion.16 = f32[64,64,64]{2,0,1:T(8,128)S(1)} fusion(f32[64,64,64]{2,1,0:T(8,128)} %reshape.238, f32[3,64,64]{2,1,0:T(8,128)S(1)} %copy-done.6), kind=kOutput, calls=%fused_computation.36 | convolution fusion | flops 201326592 | bytes 2129920 | tf_op jit(solution)/shard_map/ai,...ijk->...ajk/dot_general | solution.py:37
  43.7 5.6 %fusion.14 = f32[64,64,64]{2,1,0:T(8,128)} fusion(f32[64,64,64]{2,0,1:T(8,128)S(1)} %fusion.16, f32[3,64,64]{2,1,0:T(8,128)S(1)} %copy-done.6), kind=kOutput, calls=%fused_computation.34 | convolution fusion | flops 201326592 | bytes 3178496 | tf_op jit(solution)/shard_map/bj,...ajk->...abk/dot_general | solution.py:38
  49.3 3.3 reshape.239
  52.6 5.8 %fusion.21 = f32[64,64,64]{2,1,0:T(8,128)S(1)} fusion(f32[64,64,64]{2,1,0:T(8,128)} %reshape.239, f32[64,64,64]{2,1,0:T(8,128)} %fusion.14, f32[3,64,64]{2,1,0:T(8,128)S(1)} %copy-done.6), kind=kOutput, calls=%fused_computation.42 | convolution fusion | flops 201588736 | bytes 3178496 | tf_op jit(solution)/shard_map/ck,...abk->...abc/dot_general | solution.py:39
  58.4 5.6 %fusion.18 = f32[64,64,64]{0,2,1:T(8,128)} fusion(f32[64,64,64]{2,1,0:T(8,128)S(1)} %fusion.21, f32[3,64,64]{2,1,0:T(8,128)S(1)} %copy-done.6), kind=kOutput, calls=%fused_computation.41 | convolution fusion | flops 201326592 | bytes 3178496 | tf_op jit(solution)/shard_map/ai,...ajk->...ijk/dot_general | solution.py:43
  64.0 4.3 %copy.80 = f32[64,64,64]{1,2,0:T(8,128)} copy(f32[64,64,64]{0,2,1:T(8,128)} %fusion.18) | data formatting | bytes 2097152 | tf_op jit(solution)/shard_map/ai,...ajk->...ijk/dot_general | solution.py:43
  68.4 4.7 %fusion.40 = f32[64,64,64]{2,1,0:T(8,128)} fusion(f32[64,64,64]{1,2,0:T(8,128)} %copy.80, f32[3,64,64]{2,1,0:T(8,128)S(1)} %copy-done.6), kind=kOutput, calls=%fused_computation.73 | convolution fusion | flops 201326592 | bytes 2129920 | tf_op jit(solution)/shard_map/bj,...ibk->...ijk/dot_general | solution.py:44
  73.1 88.8 %all-reduce.6.cloned.1.call-done = f32[192,128]{1,0:T(8,128)} async-done(((f32[192,128]{1,0:T(8,128)}), f32[192,128]{1,0:T(8,128)}) %all-reduce.6.cloned.1.call-update) | async-done | bytes 98320 | tf_op jit(solution)/shard_map/psum | solution.py:95
  161.9 1.5 gather_fusion
  163.4 2.7 fusion.62
  166.1 1.6 fusion.54
  167.7 1.4 scatter_custom_fusion.1
  169.1 3.5 fusion.8
  172.7 48.9 %all-reduce.8.cloned.1.call-done = f32[24576]{0:T(1024)} async-done(((f32[24576]{0:T(1024)}), f32[24576]{0:T(1024)}) %all-reduce.8.cloned.1.call-update) | async-done | bytes 98320 | tf_op jit(solution)/shard_map/psum | solution.py:97
  221.6 37.5 %all-reduce.10.cloned.1.call-done = f32[24576]{0:T(1024)} async-done(((f32[24576]{0:T(1024)}), f32[24576]{0:T(1024)}) %all-reduce.10.cloned.1.call-update) | async-done | bytes 98320 | tf_op jit(solution)/shard_map/psum | solution.py:96
  259.1 5.0 %gather_fusion.1 = f32[768]{0:T(1024)S(1)} fusion(f32[24576]{0:T(1024)} %all-reduce.10.cloned.1.call-done, s32[1024]{0:T(1024)S(1)} %pad_clamp_fusion), kind=kCustom, calls=%fused_computation.1 | custom fusion | bytes 9216 | tf_op jit(solution)/shard_map/gather | solution.py:100
  264.1 0.7 convolution_bitcast_fusion
  265.1 0.7 copy.126
  265.8 2.1 copy.95
  267.8 5.1 %scatter-add.48 = f32[64,64,64]{1,2,0:T(8,128)S(1)} dynamic-update-slice(f32[64,64,64]{1,2,0:T(8,128)S(1)} %constant_dynamic-update-slice_fusion.2, f32[64,1,64]{1,2,0:T(8,128)} %copy.95, s32[]{:T(128)} %constant.168.clone.1, s32[]{:T(128)} %constant.168.clone.1, s32[]{:T(128)} %constant.168.clone.1) | dynamic-update-slice | bytes 32772 | tf_op jit(solution)/shard_map/scatter-add | solution.py:76
  272.9 2.0 slice.283
  274.9 2.3 copy.127
  277.1 2.1 copy.97
  279.2 8.4 %scatter-add.49 = f32[64,64,64]{1,2,0:T(8,128)S(1)} dynamic-update-slice(f32[64,64,64]{1,2,0:T(8,128)S(1)} %scatter-add.48, f32[64,1,64]{1,2,0:T(8,128)} %copy.97, s32[]{:T(128)} %constant.168.clone.1, s32[]{:T(128)} %constant.171.clone.1, s32[]{:T(128)} %constant.168.clone.1) | dynamic-update-slice | bytes 32772 | tf_op jit(solution)/shard_map/scatter-add | solution.py:77
  288.1 3.3 collective-permute-start.1
  291.3 1.3 collective-permute-start
  292.9 4.2 %collective-permute-done = f32[1,64,64]{1,2,0:T(8,128)S(1)} collective-permute-done((f32[1,64,64]{1,2,0:T(8,128)S(1)}, f32[1,64,64]{1,2,0:T(8,128)S(1)}, u32[]{:S(2)}, u32[]{:S(2)}) %collective-permute-start) | collective-permute-done | bytes 16416 | tf_op jit(solution)/shard_map/ppermute | solution.py:21
  297.3 2.8 fusion.57
  300.1 2.8 copy.104
  302.9 2.8 copy.102
  305.7 1.3 collective-permute-start.2
  307.0 3.0 collective-permute-start.3
  310.0 1.3 broadcast_add_fusion
  311.3 3.1 copy.100
  314.4 2.2 add.101
  316.6 2.9 copy.101
  319.5 3.0 copy.105
  322.6 3.1 copy.103
  325.6 3.7 select_maximum_fusion
  329.4 0.4 copy-done.4
  329.8 0.6 copy-done.5
  330.4 6.5 %multiply_reduce_fusion = (f32[]{:T(128)}, f32[]{:T(128)}, f32[64,64,64]{1,2,0:T(8,128)}) fusion(f32[64,64,64]{1,2,0:T(8,128)S(1)} %scatter-add.51, f32[64,64,64]{1,2,0:T(8,128)S(1)} %copy-done.4, f32[66,66,66]{1,2,0:T(8,128)S(1)} %select_maximum_fusion, f32[1,64,64]{1,2,0:T(8,128)S(1)} %collective-permute-done, f32[1,64,64]{1,2,0:T(8,128)S(1)} %collective-permute-done.1, ...), kind=kLoop, calls=%fused_computation.39 | loop fusion | flops 5505022 | bytes 6358024 | tf_op jit(solution)/shard_map/reduce_sum | solution.py:115
  337.0 40.2 %all-reduce.1 = (f32[]{:T(128)}, f32[]{:T(128)}) all-reduce(f32[]{:T(128)} %get-tuple-element.75, f32[]{:T(128)} %get-tuple-element.74), channel_id=1, replica_groups=mesh['sub'=4,'cgrp'=8] {'sub','cgrp'}, use_global_device_ids=true, to_apply=%region_7.0 | all-reduce | flops 2 | bytes 16 | tf_op jit(solution)/shard_map/psum | solution.py:111
  378.5 5.4 %multiply_subtract_fusion = (f32[64,64,64]{1,2,0:T(8,128)}, f32[64,64,64]{1,2,0:T(8,128)}) fusion(f32[64,64,64]{1,2,0:T(8,128)} %copy.100, f32[64,64,64]{1,2,0:T(8,128)} %get-tuple-element.80, f32[]{:T(128)S(6)} %div.3, f32[64,64,64]{1,2,0:T(8,128)S(1)} %scatter-add.51), kind=kLoop, calls=%fused_computation.38 | loop fusion | flops 786432 | bytes 5242884 | tf_op jit(solution)/shard_map/sub | solution.py:132
  383.8 1.9 copy.110
  385.7 1.6 reshape.249
  387.4 3.1 copy.108
  390.5 2.9 reshape.248
  (57 shorter events, 2.1 us)
Async XLA Ops:
  7.2 156.2 %copy-start = (f32[6,8,128,128]{3,2,1,0:T(8,128)S(1)}, f32[6,8,128,128]{3,2,1,0:T(8,128)}, u32[]{:S(2)}) copy-start(f32[6,8,128,128]{3,2,1,0:T(8,128)} %param.27) | copy-start | bytes 9437188
  7.2 154.7 %all-reduce.6.cloned.1.call-start = ((), (), s32[]{:S(2)}) async-start(), calls=%async_computation | async-start | bytes 196608 | tf_op jit(solution)/shard_map/psum | solution.py:95
  13.2 5.0 %copy-start.9 = (s32[1,1,6,128]{3,1,2,0:T(1,128)S(1)}, s32[1,1,6,128]{3,1,2,0:T(1,128)}, u32[]{:S(2)}) copy-start(s32[1,1,6,128]{3,1,2,0:T(1,128)} %param.25) | copy-start | bytes 9220
  13.2 5.0 %copy-start.7 = (f32[2,128,64]{1,2,0:T(8,128)S(1)}, f32[2,128,64]{1,2,0:T(8,128)}, u32[]{:S(2)}) copy-start(f32[2,128,64]{1,2,0:T(8,128)} %param.24) | copy-start | bytes 196612
  21.3 17.7 %copy-start.8 = (s32[6,8]{1,0:T(8,128)S(1)}, s32[6,8]{1,0:T(8,128)}, u32[]{:S(2)}) copy-start(s32[6,8]{1,0:T(8,128)} %param.26) | copy-start | bytes 580
  21.3 17.8 %copy-start.6 = (f32[3,64,64]{2,1,0:T(8,128)S(1)}, f32[3,64,64]{2,1,0:T(8,128)}, u32[]{:S(2)}) copy-start(f32[3,64,64]{2,1,0:T(8,128)} %param.23) | copy-start | bytes 147460
  38.5 183.1 %all-reduce.8.cloned.1.call-start = ((), (), s32[]{:S(2)}) async-start(), calls=%async_computation.1 | async-start | bytes 196608 | tf_op jit(solution)/shard_map/psum | solution.py:97
  169.0 90.0 %all-reduce.10.cloned.1.call-start = ((), (), s32[]{:S(2)}) async-start(), calls=%async_computation.2 | async-start | bytes 196608 | tf_op jit(solution)/shard_map/psum | solution.py:96
  288.1 4.9 %collective-permute-start.1 = (f32[1,64,64]{1,2,0:T(8,128)S(1)}, f32[1,64,64]{1,2,0:T(8,128)S(1)}, u32[]{:S(2)}, u32[]{:S(2)}) collective-permute-start(f32[1,64,64]{1,2,0:T(8,128)S(1)} %get-tuple-element.83), channel_id=1, source_target_pairs={{0,8},{8,16},{16,24},{1,9},{9,17},{17,25},{2,10},{10,18},{18,26},{... | collective-permute-start | bytes 49160 | tf_op jit(solution)/shard_map/ppermute | solution.py:20
  291.3 5.8 %collective-permute-start = (f32[1,64,64]{1,2,0:T(8,128)S(1)}, f32[1,64,64]{1,2,0:T(8,128)S(1)}, u32[]{:S(2)}, u32[]{:S(2)}) collective-permute-start(f32[1,64,64]{1,2,0:T(8,128)S(1)} %get-tuple-element.84), channel_id=1, source_target_pairs={{8,0},{16,8},{24,16},{9,1},{17,9},{25,17},{10,2},{18,10},{26,18},{... | collective-permute-start | bytes 49160 | tf_op jit(solution)/shard_map/ppermute | solution.py:21
  305.7 16.9 %collective-permute-start.2 = (f32[66,1,64]{0,2,1:T(8,128)S(1)}, f32[66,1,64]{0,2,1:T(8,128)S(1)}, u32[]{:S(2)}, u32[]{:S(2)}) collective-permute-start(f32[66,1,64]{0,2,1:T(8,128)S(1)} %copy.102), channel_id=1, source_target_pairs={{1,0},{2,1},{3,2},{4,3},{5,4},{6,5},{7,6},{9,8},{10,9},{11,10},{12... | collective-permute-start | bytes 50696 | tf_op jit(solution)/shard_map/ppermute | solution.py:21
  307.0 12.6 %collective-permute-start.3 = (f32[66,1,64]{0,2,1:T(8,128)S(1)}, f32[66,1,64]{0,2,1:T(8,128)S(1)}, u32[]{:S(2)}, u32[]{:S(2)}) collective-permute-start(f32[66,1,64]{0,2,1:T(8,128)S(1)} %copy.104), channel_id=1, source_target_pairs={{0,1},{1,2},{2,3},{3,4},{4,5},{5,6},{6,7},{8,9},{9,10},{10,11},{11... | collective-permute-start | bytes 50696 | tf_op jit(solution)/shard_map/ppermute | solution.py:20
  325.6 3.8 copy-start.2
  325.6 3.8 copy-start.3
  325.6 4.2 %copy-start.4 = (f32[64,64,64]{1,2,0:T(8,128)S(1)}, f32[64,64,64]{1,2,0:T(8,128)}, u32[]{:S(2)}) copy-start(f32[64,64,64]{1,2,0:T(8,128)} %copy.100) | copy-start | bytes 3145732
  325.6 4.8 %copy-start.5 = (f32[64,64,64]{1,2,0:T(8,128)S(1)}, f32[64,64,64]{1,2,0:T(8,128)}, u32[]{:S(2)}) copy-start(f32[64,64,64]{1,2,0:T(8,128)} %copy.101) | copy-start | bytes 3145732
  387.4 6.0 %copy-start.1 = (f32[6,8,128,128]{3,2,1,0:T(8,128)S(1)}, f32[6,8,128,128]{3,2,1,0:T(8,128)}, u32[]{:S(2)}) copy-start(f32[6,8,128,128]{3,2,1,0:T(8,128)} %param.27) | copy-start | bytes 9437188
Sparse Core Ops, SparseCore 0:
  38.6 123.2 all-reduce.5
  169.2 52.3 all-reduce.7
  224.0 35.0 all-reduce.9
